TPU v7x, 32 devices: a whole 2x2x4 slice. The times are simulated.
32 devices in a mesh: rows: 8 (over y, x, core), ch: 4 (over z).
Axes of the slice: x: 2, y: 2, z: 4, core: 2. Of those that a mesh axis runs over, the one named last changes fastest.
Arguments:
- field: float32 [2, 128, 32, 1024], P(None, 'ch', 'rows'), may hold values from -6 to 6
- cotangent: float32 [2, 128, 32, 1024], P(None, 'ch', 'rows'), may hold values from -3 to 3
- weight: float32 [32, 128, 128, 128], P('rows', 'ch'), may hold values from -0.75 to 0.75
- bias: float32 [128], replicated, may hold values from -3 to 3
- mode_rows: int32 [32], replicated, may hold values from 0 to 31, as said below
- mode_cols: int32 [64], replicated, may hold values from 0 to 1023, as said below
Outputs:
- grad_field: float32 [2, 128, 32, 1024], P(None, 'ch', 'rows')
- grad_weight: float32 [32, 128, 128, 128], P('rows', 'ch')
Inputs may be any that keep to these rules, and one draw needn't show every extreme that they name: `mode_rows`: 32 distinct values; 0 and 31 are among them. `mode_cols`: 64 distinct values; 0 and 1023 are among them.
All inputs are finite; a program needn't handle non-finite values.
Results may differ from a plain program's by a relative error of at most 0.0003.
Values sent between devices are 32-bit elements; how exact they have to be, the bound alone decides.
A program may use at most 64 MiB of HBM per device.

v0:
```python
import functools
import math

import jax
import jax.numpy as jnp
from jax import lax
from jax.experimental import pallas as pl
from jax.experimental.pallas import tpu as pltpu
from jax.sharding import PartitionSpec as P

precise_mode = lax.Precision.HIGHEST


def angle_table(modes, positions, length):
    phase = modes[:, None] * positions[None, :] % length
    return phase.astype(jnp.float32) * (2.0 * math.pi / length)


def column_table(mode_cols, length):
    angles = angle_table(mode_cols, jnp.arange(length, dtype=jnp.int32), length)
    stacked = jnp.stack([jnp.cos(angles), -jnp.sin(angles)], axis=1)
    return stacked.reshape(2 * mode_cols.shape[0], length)


def row_table(modes, positions, length):
    angles = angle_table(modes, positions, length)
    return jnp.concatenate([jnp.cos(angles), jnp.sin(angles)], axis=0)


def split_parts(values):
    shaped = values.reshape(values.shape[:-1] + (values.shape[-1] // 2, 2))
    return (shaped[..., 0], shaped[..., 1])


def join_parts(real, imag):
    return jnp.stack([real, imag], axis=-1).reshape(real.shape[:-1] + (2 * real.shape[-1],))


def analyze_rows(columns, table):
    count = table.shape[0] // 2
    shaped = columns.reshape(columns.shape[:-1] + (columns.shape[-1] // 2, 2))
    both = jnp.einsum("kh,bchmp->kbcmp", table, shaped, precision=precise_mode)
    cosine, sine = (both[:count], both[count:])
    return join_parts(cosine[..., 0] + sine[..., 1], cosine[..., 1] - sine[..., 0])


def synth_rows(modes, table):
    count = modes.shape[0]
    shaped = modes.reshape(modes.shape[:-1] + (modes.shape[-1] // 2, 2))
    cosine = jnp.einsum("kh,kbomp->bohmp", table[:count], shaped, precision=precise_mode)
    sine = jnp.einsum("kh,kbomp->bohmp", table[count:], shaped, precision=precise_mode)
    return join_parts(cosine[..., 0] - sine[..., 1], cosine[..., 1] + sine[..., 0])


def mix_modes(spectrum, weight):
    spec_re, spec_im = split_parts(spectrum)
    wgt_re, wgt_im = split_parts(weight)

    def contract(left, right):
        return jnp.einsum("kbcm,kcom->kbom", left, right, precision=precise_mode)

    real = contract(spec_re, wgt_re) - contract(spec_im, wgt_im)
    imag = contract(spec_re, wgt_im) + contract(spec_im, wgt_re)
    return join_parts(real, imag)


def mix_grads(spectrum, weight, grad_mixed):
    spec_re, spec_im = split_parts(spectrum)
    wgt_re, wgt_im = split_parts(weight)
    grad_re, grad_im = split_parts(grad_mixed)

    def outer(left, right):
        return jnp.einsum("kbom,kbcm->kcom", left, right, precision=precise_mode)

    def inner(left, right):
        return jnp.einsum("kcom,kbom->kbcm", left, right, precision=precise_mode)

    weight_re = outer(grad_re, spec_re) + outer(grad_im, spec_im)
    weight_im = outer(grad_im, spec_re) - outer(grad_re, spec_im)
    input_re = inner(wgt_re, grad_re) + inner(wgt_im, grad_im)
    input_im = inner(wgt_re, grad_im) - inner(wgt_im, grad_re)
    return (join_parts(weight_re, weight_im), join_parts(input_re, input_im))


def gelu_slope(values):
    cumulative = 0.5 * (1.0 + jax.scipy.special.erf(values / math.sqrt(2.0)))
    density = jnp.exp(-0.5 * values * values) / math.sqrt(2.0 * math.pi)
    return cumulative + values * density


def body(field, cotangent, weight, bias, mode_rows, mode_cols):
    rows_here = field.shape[2]
    row_count = lax.axis_size("rows")
    grid_rows = rows_here * row_count
    grid_cols = field.shape[3]
    all_rows = jnp.arange(grid_rows, dtype=jnp.int32)
    table_w = column_table(mode_cols, grid_cols)
    scale_fwd = 1.0 / math.sqrt(grid_rows * grid_cols)
    scale_inv = 1.0 / math.sqrt(mode_rows.shape[0] * mode_cols.shape[0])

    def analyze(values):
        columns = jnp.dot(
            values, table_w.T, precision=precise_mode, preferred_element_type=jnp.float32
        )
        spread = lax.all_to_all(columns, "rows", split_axis=3, concat_axis=2, tiled=True)
        pieces = analyze_rows(spread, row_table(mode_rows, all_rows, grid_rows))
        return lax.all_to_all(pieces, "rows", split_axis=0, concat_axis=3, tiled=True)

    def synthesize(modes):
        spread = lax.all_to_all(modes, "rows", split_axis=3, concat_axis=0, tiled=True)
        pieces = synth_rows(spread, row_table(mode_rows, all_rows, grid_rows))
        gathered = lax.all_to_all(pieces, "rows", split_axis=2, concat_axis=3, tiled=True)
        return jnp.dot(
            gathered, table_w, precision=precise_mode, preferred_element_type=jnp.float32
        )

    spectrum = analyze(field) * scale_fwd
    mixed = lax.psum_scatter(mix_modes(spectrum, weight), "ch", scatter_dimension=2, tiled=True)
    outputs_here = mixed.shape[2]
    bias_here = lax.dynamic_slice_in_dim(bias, lax.axis_index("ch") * outputs_here, outputs_here)
    before = synthesize(mixed) * scale_inv + bias_here[None, :, None, None]
    grad_before = cotangent * gelu_slope(before)
    grad_mixed = analyze(grad_before) * scale_inv
    grad_whole = lax.all_gather(grad_mixed, "ch", axis=2, tiled=True)
    grad_weight, grad_spectrum = mix_grads(spectrum, weight, grad_whole)
    grad_field = synthesize(grad_spectrum) * scale_fwd
    return (grad_field, grad_weight)


def split_bf16(values):
    high = values.astype(jnp.bfloat16)
    low = (values - high.astype(jnp.float32)).astype(jnp.bfloat16)
    return high, low


def turn_cosine(step, length):
    step = lax.rem(step, jnp.int32(length)) if length & (length - 1) else step & (length - 1)
    folded = jnp.abs(step - length // 2) - length // 4
    angle = folded.astype(jnp.float32) * (2.0 * math.pi / length)
    square = angle * angle
    total = jnp.float32(-2.5052108e-08)
    for factor in (2.7557319e-06, -1.9841270e-04, 8.3333333e-03, -1.6666667e-01):
        total = total * square + factor
    return angle + angle * square * total


def next_lane(values):
    return pltpu.roll(values, values.shape[-1] - 1, values.ndim - 1)


def prev_lane(values):
    return pltpu.roll(values, 1, values.ndim - 1)


def even_lanes(values):
    return lax.broadcasted_iota(jnp.int32, values.shape, values.ndim - 1) % 2 == 0


def swap_pairs(values):
    return jnp.where(even_lanes(values), next_lane(values), prev_lane(values))


def layer_kernel(
    sizes, field_hbm, cot_hbm, weight_hbm, bias_hbm, colmode_hbm, rowmode_hbm,
    gfield_hbm, same_ref, cross_ref, grads_ref, gswap_ref,
    weight_ref, field_ref, cot_ref, gfield_ref, bias_ref, colmode_ref, rowmode_ref,
    high_ref, low_ref, fwd_ref, inv_ref, stack_ref,
    few_ref, many_ref, part_ref, arrive_ref, gall_ref, accp_ref, accq_ref,
    local_sem, field_sem, send_sem, recv_sem, ch_send, ch_recv,
):
    samples, chans, rows_here, width, kept, ranks, groups, lanes = sizes
    grid_rows = rows_here * ranks
    kept_here = kept // ranks
    handlers = ranks // samples
    own_chans = chans // handlers
    flat_rows = chans * rows_here
    scale_fwd = 1.0 / math.sqrt(grid_rows * width)
    scale_inv = 1.0 / math.sqrt(kept * (lanes // 2))
    me, mine = lax.axis_index("rows"), lax.axis_index("ch")
    my_sample, my_slot = lax.rem(me, samples), me // samples
    mesh_ids = pl.DeviceIdType.MESH

    def rank_at(step):
        return lax.rem(me + step, ranks)

    def group_at(step):
        return lax.rem(mine + step, groups)

    barrier = pltpu.get_barrier_semaphore()
    for step in range(1, ranks):
        pl.semaphore_signal(barrier, inc=1, device_id=(rank_at(step), mine), device_id_type=mesh_ids)
    for step in range(1, groups):
        pl.semaphore_signal(barrier, inc=1, device_id=(me, group_at(step)), device_id_type=mesh_ids)

    loads = []
    for at, (source, target) in enumerate((
        (colmode_hbm, colmode_ref), (rowmode_hbm, rowmode_ref), (bias_hbm, bias_ref),
    )):
        load = pltpu.make_async_copy(source, target, local_sem.at[at])
        load.start()
        loads.append(load)

    def row_copies(source, target, kind):
        found = []
        for b in range(samples):
            for h in range(rows_here):
                copy = pltpu.make_async_copy(
                    source.at[b, :, h, :], target.at[b, h], field_sem.at[kind, b, h]
                )
                copy.start()
                found.append(copy)
        return found

    load_field = row_copies(field_hbm, field_ref, 0)
    load_weight = pltpu.make_async_copy(weight_hbm, weight_ref, local_sem.at[3])
    load_weight.start()
    load_cot = row_copies(cot_hbm, cot_ref, 1)
    for load in loads:
        load.wait()

    def as_column(values):
        count = values.shape[1]
        row = lax.broadcasted_iota(jnp.int32, (count, count), 0)
        lane = lax.broadcasted_iota(jnp.int32, (count, count), 1)
        kept_values = jnp.where(row == lane, values.astype(jnp.float32), 0.0)
        return jnp.sum(kept_values, axis=1, keepdims=True)

    def pick(column, index):
        row = lax.broadcasted_iota(jnp.int32, (column.shape[0], index.shape[1]), 0)
        return jnp.sum(jnp.where(row == index, column, 0.0), axis=0, keepdims=True).astype(jnp.int32)

    col_column = as_column(colmode_ref[...])
    col_lanes = pick(col_column, lax.broadcasted_iota(jnp.int32, (1, lanes), 1) // 2)
    row_column = as_column(rowmode_ref[...])
    row_lanes = pick(row_column, lax.broadcasted_iota(jnp.int32, (1, 6 * kept), 1) % kept)
    row_column = row_column.astype(jnp.int32)
    chunk = 128

    @pl.loop(0, width // chunk)
    def _(at):
        shape = (chunk, lanes)
        column = lax.broadcasted_iota(jnp.int32, shape, 0) + at * chunk
        quarter = lax.broadcasted_iota(jnp.int32, shape, 1) % 2 * (width // 4)
        high, low = split_bf16(turn_cosine(col_lanes * column + quarter, width))
        here = pl.ds(pl.multiple_of(at * chunk, chunk), chunk)
        high_ref[here, :] = high
        low_ref[here, :] = low

    def packed_table(step, length):
        table = turn_cosine(step, length)
        high, low = split_bf16(table)
        lane = lax.broadcasted_iota(jnp.int32, table.shape, 1)
        edge = table.shape[1] // 3 * 2
        chosen = jnp.where(lane < edge, high.astype(jnp.float32), low.astype(jnp.float32))
        return chosen.astype(jnp.bfloat16)

    spot = lax.broadcasted_iota(jnp.int32, (kept, 6 * grid_rows), 1)
    turn = spot // grid_rows % 2 * (3 * grid_rows // 4)
    fwd_ref[...] = packed_table(row_column * (spot % grid_rows) + turn, grid_rows)
    spot = lax.broadcasted_iota(jnp.int32, (grid_rows, 6 * kept), 1)
    turn = spot // kept % 2 * (grid_rows // 4)
    row = lax.broadcasted_iota(jnp.int32, (grid_rows, 6 * kept), 0)
    inv_ref[...] = packed_table(row_lanes * row + turn, grid_rows)
    whole = bias_ref.shape[1]
    out_chan = mine * chans + lax.broadcasted_iota(jnp.int32, (flat_rows, whole), 0) % chans
    picked = lax.broadcasted_iota(jnp.int32, (flat_rows, whole), 1) == out_chan
    bias_rows = jnp.sum(jnp.where(picked, bias_ref[...], 0.0), axis=1, keepdims=True)

    def column_product(values, contract):
        high, low = split_bf16(values)
        dims = (((1,), (contract,)), ((), ()))

        def product(left, right):
            return lax.dot_general(left, right, dims, preferred_element_type=jnp.float32)

        return (
            product(high, low_ref[...]) + product(low, high_ref[...]) + product(high, high_ref[...])
        )

    def analyze_cols(values):
        result = column_product(values.reshape(flat_rows, width), 0)
        return result.reshape(rows_here, chans, lanes)

    def synth_cols(values):
        return column_product(values.reshape(flat_rows, lanes), 1)

    def block(rank, size):
        return pl.ds(pl.multiple_of(rank * size, size), size)

    def row_copy(phase, source, target, peer, origin):
        return pltpu.make_async_remote_copy(
            src_ref=source, dst_ref=target,
            send_sem=send_sem.at[phase, peer], recv_sem=recv_sem.at[phase, origin],
            device_id=(peer, mine), device_id_type=mesh_ids,
        )

    at_end = []

    def spread(phase, b):
        few, many = few_ref.at[phase, b], many_ref.at[phase]
        size = few.shape[0]

        def copy_to(slot):
            return row_copy(
                phase, few.at[:, block(slot, own_chans), :], many.at[block(me, size)],
                slot * samples + b, me,
            )

        def each(act):
            for step in range(1, handlers):
                act(copy_to(lax.rem(my_slot + step, handlers)))

            @pl.when(my_sample != b)
            def _():
                act(copy_to(my_slot))

        each(lambda copy: copy.start())
        at_end.append(lambda: each(lambda copy: copy.wait_send()))

        @pl.when(my_sample == b)
        def _():
            many[block(me, size)] = few[:, block(my_slot, own_chans), :]

    def transform(phase, b, table_ref, scale):
        @pl.when(my_sample == b)
        def _():
            source, result_ref = many_ref.at[phase], many_ref.at[phase + 1]
            count = source.shape[0]
            size = count // ranks
            for step in range(1, ranks):
                origin = rank_at(step)
                here = source.at[block(origin, size)]
                row_copy(phase, here, here, origin, origin).wait_recv()
            for pair in range(own_chans):
                values = source[:, pair, :]
                crossed = jnp.where(even_lanes(values), next_lane(values), -prev_lane(values))
                here = slice(pair * lanes, (pair + 1) * lanes)
                for at, piece in enumerate((values, crossed)):
                    high, low = split_bf16(piece)
                    stack_ref[at * count:(at + 1) * count, here] = high
                    stack_ref[(2 + at) * count:(3 + at) * count, here] = low
                    stack_ref[(4 + at) * count:(5 + at) * count, here] = high
            result = jnp.dot(table_ref[...], stack_ref[...], preferred_element_type=jnp.float32)
            result = result * scale
            for pair in range(own_chans):
                result_ref[:, pair, :] = result[:, pair * lanes:(pair + 1) * lanes]
            few = few_ref.at[phase + 1, b]
            for step in range(1, ranks):
                peer = rank_at(step)
                row_copy(
                    phase + 1, result_ref.at[block(peer, size)],
                    few.at[:, block(my_slot, own_chans), :], peer, me,
                ).start()
            few[:, block(my_slot, own_chans), :] = result_ref[block(me, size)]

        def finish():
            @pl.when(my_sample == b)
            def _():
                size = many_ref.shape[1] // ranks
                for step in range(1, ranks):
                    peer = rank_at(step)
                    here = many_ref.at[phase + 1, block(peer, size)]
                    row_copy(phase + 1, here, here, peer, me).wait_send()

        at_end.append(finish)

    def collected(phase, b):
        few = few_ref.at[phase, b]

        def arrived(slot):
            here = few.at[:, block(slot, own_chans), :]
            origin = slot * samples + b
            row_copy(phase, here, here, origin, origin).wait_recv()

        for step in range(1, handlers):
            arrived(lax.rem(my_slot + step, handlers))

        @pl.when(my_sample != b)
        def _():
            arrived(my_slot)

        return few

    def mix_group(b, group, out_ref):
        outs = pl.ds(pl.multiple_of(group * chans, chans), chans)

        @pl.loop(0, kept_here)
        def _(k):
            plain = jnp.zeros((chans, lanes), jnp.float32)
            turned = jnp.zeros((chans, lanes), jnp.float32)
            for c in range(chans):
                w = weight_ref[k, c, outs, :]
                at = b * chans + c
                plain = plain + w * same_ref[k, at:at + 1, :]
                turned = turned + w * cross_ref[k, at:at + 1, :]
            out_ref[k] = plain + swap_pairs(turned)

    def group_copy(kind, b, step, source, target):
        return pltpu.make_async_remote_copy(
            src_ref=source, dst_ref=target,
            send_sem=ch_send.at[kind, b, step - 1], recv_sem=ch_recv.at[kind, b, step - 1],
            device_id=(me, group_at(step)), device_id_type=mesh_ids,
        )

    order = sorted(range(1, groups), key=lambda step: -min(step, groups - step))
    tile = 8

    def back_group(b, group, grad_ref, fresh):
        here = slice(b * chans, (b + 1) * chans)
        for k in range(kept_here):
            values = grad_ref[k]
            grads_ref[group, k, here, :] = values
            gswap_ref[group, k, here, :] = swap_pairs(values)

        @pl.loop(0, kept_here * (chans // tile))
        def _(at):
            k, first = at // (chans // tile), at % (chans // tile) * tile
            sums = [[None, None] for _ in range(tile)]
            for o in range(0, chans, tile):
                row = slice(b * chans + o, b * chans + o + tile)
                factors = (grads_ref[group, k, row, :], gswap_ref[group, k, row, :])
                outs = pl.ds(pl.multiple_of(group * chans + o, tile), tile)
                for c in range(tile):
                    w = weight_ref[k, first + c, outs, :]
                    for i, factor in enumerate(factors):
                        term = w * factor
                        sums[c][i] = term if sums[c][i] is None else sums[c][i] + term
            into = pl.ds(pl.multiple_of(first, tile), tile)
            for i, acc_ref in ((0, accp_ref), (1, accq_ref)):
                rows = [jnp.sum(sums[c][i], axis=0, keepdims=True) for c in range(tile)]
                total = jnp.concatenate(rows, axis=0)
                acc_ref[b, k, into, :] = total if fresh else acc_ref[b, k, into, :] + total

    def flow(b):
        for copy in load_field[b * rows_here:(b + 1) * rows_here]:
            copy.wait()
        few_ref[0, b] = analyze_cols(field_ref[b])
        if b == 0:
            pl.semaphore_wait(barrier, ranks - 1 + groups - 1)
        spread(0, b)
        yield
        transform(0, b, fwd_ref, scale_fwd)
        yield
        spectrum = collected(1, b)
        here = slice(b * chans, (b + 1) * chans)
        for k in range(kept_here):
            values = spectrum[k]
            even = even_lanes(values)
            same_ref[k, here, :] = jnp.where(even, values, prev_lane(values))
            cross_ref[k, here, :] = jnp.where(even, next_lane(values), -values)
        if b == 0:
            load_weight.wait()
        copies = []
        for step in order:
            part = part_ref.at[b, step - 1]
            mix_group(b, group_at(step), part)
            copy = group_copy(0, b, step, part, arrive_ref.at[b, step - 1])
            copy.start()
            copies.append(copy)
        mixed = few_ref.at[2, b]
        mix_group(b, mine, mixed)
        at_end.extend(copy.wait_send for copy in copies)
        yield
        for copy in copies:
            copy.wait_recv()
        for k in range(kept_here):
            total = mixed[k]
            for step in order:
                total = total + arrive_ref[b, step - 1, k]
            mixed[k] = total
        spread(2, b)
        yield
        transform(2, b, inv_ref, scale_inv)
        yield
        few = collected(3, b)
        for copy in load_cot[b * rows_here:(b + 1) * rows_here]:
            copy.wait()
        before = synth_cols(few[...]) + bias_rows
        slope = 0.5 * (1.0 + lax.erf(before * (1.0 / math.sqrt(2.0))))
        slope = slope + before * jnp.exp(-0.5 * before * before) * (1.0 / math.sqrt(2.0 * math.pi))
        few_ref[4, b] = analyze_cols(cot_ref[b].reshape(flat_rows, width) * slope)
        spread(4, b)
        yield
        transform(4, b, fwd_ref, scale_inv)
        yield
        own = collected(5, b)
        copies = []
        for step in order:
            copy = group_copy(1, b, step, own, gall_ref.at[b, mine])
            copy.start()
            copies.append(copy)
        at_end.extend(copy.wait_send for copy in copies)
        back_group(b, mine, own, True)
        yield
        for step in sorted(order, key=lambda step: min(step, groups - step)):
            copies[order.index(step)].wait_recv()
            source = lax.rem(mine + groups - step, groups)
            back_group(b, source, gall_ref.at[b, source], False)
        for k in range(kept_here):
            p, q = accp_ref[b, k], accq_ref[b, k]
            few_ref[6, b, k] = jnp.where(even_lanes(p), p + next_lane(p), prev_lane(q) - q)
        spread(6, b)
        yield
        transform(6, b, inv_ref, scale_fwd)
        yield
        few = collected(7, b)
        gfield_ref[b] = synth_cols(few[...]).reshape(rows_here, chans, width)
        for h in range(rows_here):
            copy = pltpu.make_async_copy(
                gfield_ref.at[b, h], gfield_hbm.at[b, :, h, :], field_sem.at[0, b, h]
            )
            copy.start()
            at_end.append(copy.wait)

    flows = [flow(b) for b in range(samples)]
    while flows:
        for one in list(flows):
            if next(one, flows) is flows:
                flows.remove(one)
    for act in at_end:
        act()


def weight_kernel(chans, samples, same_ref, cross_ref, grads_ref, gswap_ref, out_ref):
    tile, together = 8, 2
    count = out_ref.shape[1]
    first = pl.program_id(1) * count

    for c in range(0, count, together):
        same, cross = [
            [
                [ref[0, pl.ds(b * chans + first + c + i, 1), :] for b in range(samples)]
                for i in range(together)
            ]
            for ref in (same_ref, cross_ref)
        ]
        for group in range(grads_ref.shape[0]):
            for o in range(0, chans, tile):
                rows = [slice(b * chans + o, b * chans + o + tile) for b in range(samples)]
                plain = [grads_ref[group, 0, row, :] for row in rows]
                turned = [gswap_ref[group, 0, row, :] for row in rows]
                at = group * chans + o
                for i in range(together):
                    total = plain[0] * same[i][0] + turned[0] * cross[i][0]
                    for b in range(1, samples):
                        total = total + plain[b] * same[i][b] + turned[b] * cross[i][b]
                    out_ref[0, c + i, at:at + tile, :] = total


def kernel_fits(ranks, groups, field, weight, mode_rows, bias):
    pairs = field.shape[0] * field.shape[1]
    lanes = weight.shape[3]
    return (
        pairs % (8 * ranks) == 0 and ranks % field.shape[0] == 0 and lanes == 128 and field.shape[1] % 8 == 0
        and field.shape[1] * groups == weight.shape[2] and mode_rows.shape[0] % 32 == 0
        and field.shape[2] * ranks % 32 == 0 and mode_rows.shape[0] == field.shape[2] * ranks
        and field.shape[3] % 128 == 0 and bias.shape[0] % 128 == 0
    )


def kernel_body(field, cotangent, weight, bias, mode_rows, mode_cols):
    samples, chans, rows_here, width = field.shape
    ranks, groups = lax.axis_size("rows"), lax.axis_size("ch")
    kept, lanes = mode_rows.shape[0], weight.shape[3]
    grid_rows = rows_here * ranks
    kept_here = kept // ranks
    pairs = samples * chans
    own_chans = pairs // ranks
    f32, bf16, i32 = jnp.float32, jnp.bfloat16, jnp.int32
    sizes = (samples, chans, rows_here, width, kept, ranks, groups, lanes)
    vmem = pl.BlockSpec(memory_space=pltpu.VMEM)
    hbm = pl.BlockSpec(memory_space=pl.ANY)
    modes = (kept_here, pairs, lanes)
    slab = (kept_here, chans, lanes)
    by_row = (samples, rows_here, chans, width)
    dma = pltpu.SemaphoreType.DMA
    gfield, same, cross, grads, gswap = pl.pallas_call(
        functools.partial(layer_kernel, sizes),
        out_shape=(
            jax.ShapeDtypeStruct(field.shape, f32),
            jax.ShapeDtypeStruct(modes, f32),
            jax.ShapeDtypeStruct(modes, f32),
            jax.ShapeDtypeStruct((groups,) + modes, f32),
            jax.ShapeDtypeStruct((groups,) + modes, f32),
        ),
        in_specs=[hbm] * 6,
        out_specs=(hbm,) + (vmem,) * 4,
        scratch_shapes=[
            pltpu.VMEM(weight.shape, f32),
            pltpu.VMEM(by_row, f32),
            pltpu.VMEM(by_row, f32),
            pltpu.VMEM(by_row, f32),
            pltpu.VMEM((1, bias.shape[0]), f32),
            pltpu.VMEM((1, lanes // 2), i32),
            pltpu.VMEM((1, kept), i32),
            pltpu.VMEM((width, lanes), bf16),
            pltpu.VMEM((width, lanes), bf16),
            pltpu.VMEM((kept, 6 * grid_rows), bf16),
            pltpu.VMEM((grid_rows, 6 * kept), bf16),
            pltpu.VMEM((6 * kept, own_chans * lanes), bf16),
            pltpu.VMEM((8, samples) + slab, f32),
            pltpu.VMEM((8, grid_rows, own_chans, lanes), f32),
            pltpu.VMEM((samples, groups - 1) + slab, f32),
            pltpu.VMEM((samples, groups - 1) + slab, f32),
            pltpu.VMEM((samples, groups) + slab, f32),
            pltpu.VMEM((samples,) + slab, f32),
            pltpu.VMEM((samples,) + slab, f32),
            dma((4,)),
            dma((2, samples, rows_here)),
            dma((8, ranks)),
            dma((8, ranks)),
            dma((2, samples, groups - 1)),
            dma((2, samples, groups - 1)),
        ],
        compiler_params=pltpu.CompilerParams(
            collective_id=0, has_side_effects=True, vmem_limit_bytes=52 * 1024 * 1024
        ),
    )(
        field, cotangent, weight,
        bias.reshape(1, bias.shape[0]),
        mode_cols.reshape(1, lanes // 2),
        mode_rows.reshape(1, kept),
    )
    count = 8
    one = pl.BlockSpec((1, pairs, lanes), lambda k, c: (k, 0, 0))
    every = pl.BlockSpec((groups, 1, pairs, lanes), lambda k, c: (0, k, 0, 0))
    gweight = pl.pallas_call(
        functools.partial(weight_kernel, chans, samples),
        out_shape=jax.ShapeDtypeStruct(weight.shape, f32),
        grid=(kept_here, chans // count),
        in_specs=[one, one, every, every],
        out_specs=pl.BlockSpec((1, count) + weight.shape[2:], lambda k, c: (k, c, 0, 0)),
        compiler_params=pltpu.CompilerParams(vmem_limit_bytes=32 * 1024 * 1024),
    )(same, cross, grads, gswap)
    return gfield, gweight


def any_body(field, cotangent, weight, bias, mode_rows, mode_cols):
    ranks, groups = lax.axis_size("rows"), lax.axis_size("ch")
    chosen = kernel_body if kernel_fits(ranks, groups, field, weight, mode_rows, bias) else body
    return chosen(field, cotangent, weight, bias, mode_rows, mode_cols)


def solution(mesh):
    return jax.shard_map(
        any_body,
        mesh=mesh,
        in_specs=(
            P(None, "ch", "rows", None),
            P(None, "ch", "rows", None),
            P("rows", "ch", None, None),
            P(),
            P(),
            P(),
        ),
        out_specs=(P(None, "ch", "rows", None), P("rows", "ch", None, None)),
        check_vma=False,
    )
```

profile of v0, /device:TPU:17, one launch (start us, length us, event | category | flops | bytes accessed | tf_op | source)
XLA Modules:
  0.0 72.2 jit_solution(6897467451851747445)
XLA Ops:
  0.6 0.0 copy-start
  0.6 0.6 copy-done
  1.3 0.0 copy-start.1
  1.3 0.7 copy-done.1
  1.9 0.0 copy-start.2
  1.9 0.7 copy-done.2
  2.6 61.0 %shard_map.77 = (f32[2,32,4,1024]{3,2,1,0:T(4,128)}, f32[4,64,128]{2,1,0:T(8,128)S(1)}, f32[4,64,128]{2,1,0:T(8,128)S(1)}, f32[4,4,64,128]{3,2,1,0:T(8,128)S(1)}, f32[4,4,64,128]{3,2,1,0:T(8,128)S(1)}) custom-call(f32[2,32,4,1024]{3,2,1,0:T(4,128)} %field_hbm.1, f32[2,32,4,1024]{3,2,1,0:T(4,128)} %cot_hbm.1, f32[4,32,128,128]{3,2,1,0:T(8,128)} %weight_hbm.1, ...), custom_call_target="tpu_custom_call" | custom-call | tf_op jit(solution)/shard_map/pallas_call | solution.py:577
  63.6 0.0 copy-start.3
  63.6 7.7 %shard_map.78 = f32[4,32,128,128]{3,2,1,0:T(8,128)} custom-call(f32[4,64,128]{2,1,0:T(8,128)S(1)} %get-tuple-element.8.same_ref, f32[4,64,128]{2,1,0:T(8,128)S(1)} %get-tuple-element.9.cross_ref, f32[4,4,64,128]{3,2,1,0:T(8,128)S(1)} %get-tuple-element.10.grads_ref, f32[4,4,64,128]{3,2,1,0:T(8,128)S(1)} %get-tuple-element.11.gswap_ref), custom_call_target="tpu_custom_call" | custom-call | tf_op jit(solution)/shard_map/pallas_call | solution.py:627
  71.2 0.0 copy-done.3
  71.2 1.0 %copy.9 = f32[2,32,4,1024]{3,2,1,0:T(4,128)} copy(f32[2,32,4,1024]{3,2,1,0:T(4,128)S(1)} %copy-done.3) | data formatting | bytes 2097152
Async XLA Ops:
  0.6 0.7 copy-start
  1.3 0.7 copy-start.1
  1.9 0.7 copy-start.2
  63.6 7.7 %copy-start.3 = (f32[2,32,4,1024]{3,2,1,0:T(4,128)S(1)}, f32[2,32,4,1024]{3,2,1,0:T(4,128)}, u32[]{:S(2)}) copy-start(f32[2,32,4,1024]{3,2,1,0:T(4,128)} %get-tuple-element.14) | copy-start | bytes 3145732
where the time goes:
time: 72.9 us; the launch traced here: 72.2 us
  Pallas kernels  68.6 us (94%)
  local copies, waits for them, and re-layouts  2.93 us (4%)
    pallas_call x1, Pallas kernels, kernel_body(): pl.pallas_call(functools.partial(layer_kernel, sizes), out_shape=(jax.Sha...  61 us
    pallas_call x1, Pallas kernels, kernel_body(): pl.pallas_call(functools.partial(weight_kernel, chans, samples), out_shap...  7.66 us
    unnamed x9, local copies, waits for them, and re-layouts  2.93 us

commit v1 on v0

--- a/solution.py
+++ b/solution.py
@@ -160,12 +160,34 @@
     return jnp.where(even_lanes(values), next_lane(values), prev_lane(values))
 
 
+def swap_rows(values, distance):
+    row = lax.broadcasted_iota(jnp.int32, values.shape, 0)
+    ahead = pltpu.roll(values, values.shape[0] - distance, 0)
+    behind = pltpu.roll(values, distance, 0)
+    return jnp.where(row // distance % 2 == 0, ahead, behind)
+
+
+def row_sums(tiles):
+    count = len(tiles)
+    row = lax.broadcasted_iota(jnp.int32, tiles[0].shape, 0)
+    while len(tiles) > 1:
+        half = len(tiles) // 2
+        first = row // half % 2 == 0
+        merged = []
+        for one, two in zip(tiles[:half], tiles[half:]):
+            stay, move = jnp.where(first, one, two), jnp.where(first, two, one)
+            moved = pltpu.roll(move, half, 0) if 2 * half == count else swap_rows(move, half)
+            merged.append(stay + moved)
+        tiles = merged
+    return tiles[0]
+
+
 def layer_kernel(
     sizes, field_hbm, cot_hbm, weight_hbm, bias_hbm, colmode_hbm, rowmode_hbm,
-    gfield_hbm, same_ref, cross_ref, grads_ref, gswap_ref,
-    weight_ref, field_ref, cot_ref, gfield_ref, bias_ref, colmode_ref, rowmode_ref,
-    high_ref, low_ref, fwd_ref, inv_ref, stack_ref,
-    few_ref, many_ref, part_ref, arrive_ref, gall_ref, accp_ref, accq_ref,
+    gfield_ref, same_ref, cross_ref, grads_ref, gswap_ref,
+    weight_ref, field_ref, cot_ref, bias_ref, colmode_ref, rowmode_ref,
+    analysis_ref, synthesis_ref, fwd_ref, inv_ref, stack_ref,
+    few_ref, many_ref, part_ref, arrive_ref, gall_ref, acc_ref,
     local_sem, field_sem, send_sem, recv_sem, ch_send, ch_recv,
 ):
     samples, chans, rows_here, width, kept, ranks, groups, lanes = sizes
@@ -243,8 +265,22 @@
         quarter = lax.broadcasted_iota(jnp.int32, shape, 1) % 2 * (width // 4)
         high, low = split_bf16(turn_cosine(col_lanes * column + quarter, width))
         here = pl.ds(pl.multiple_of(at * chunk, chunk), chunk)
-        high_ref[here, :] = high
-        low_ref[here, :] = low
+        analysis_ref[here, :lanes] = high
+        analysis_ref[here, lanes:] = low
+
+    def fill_synthesis():
+        modes = as_column(col_lanes).astype(jnp.int32)
+
+        @pl.loop(0, width // chunk)
+        def _(at):
+            shape = (lanes, chunk)
+            column = lax.broadcasted_iota(jnp.int32, shape, 1) + at * chunk
+            quarter = lax.broadcasted_iota(jnp.int32, shape, 0) % 2 * (width // 4)
+            high, low = split_bf16(turn_cosine(modes * column + quarter, width))
+            here = pl.ds(pl.multiple_of(at * chunk, chunk), chunk)
+            synthesis_ref[:lanes, here] = high
+            synthesis_ref[lanes:2 * lanes, here] = low
+            synthesis_ref[2 * lanes:, here] = high
 
     def packed_table(step, length):
         table = turn_cosine(step, length)
@@ -266,23 +302,19 @@
     picked = lax.broadcasted_iota(jnp.int32, (flat_rows, whole), 1) == out_chan
     bias_rows = jnp.sum(jnp.where(picked, bias_ref[...], 0.0), axis=1, keepdims=True)
 
-    def column_product(values, contract):
-        high, low = split_bf16(values)
-        dims = (((1,), (contract,)), ((), ()))
-
-        def product(left, right):
-            return lax.dot_general(left, right, dims, preferred_element_type=jnp.float32)
-
-        return (
-            product(high, low_ref[...]) + product(low, high_ref[...]) + product(high, high_ref[...])
+    def analyze_cols(values):
+        high, low = split_bf16(values.reshape(flat_rows, width))
+        both = jnp.concatenate([high, low], axis=0)
+        result = jnp.dot(both, analysis_ref[...], preferred_element_type=jnp.float32)
+        top = result[:flat_rows, :lanes] + (
+            result[:flat_rows, lanes:] + result[flat_rows:, :lanes]
         )
-
-    def analyze_cols(values):
-        result = column_product(values.reshape(flat_rows, width), 0)
-        return result.reshape(rows_here, chans, lanes)
+        return top.reshape(rows_here, chans, lanes)
 
     def synth_cols(values):
-        return column_product(values.reshape(flat_rows, lanes), 1)
+        high, low = split_bf16(values.reshape(flat_rows, lanes))
+        packed = jnp.concatenate([high, high, low], axis=1)
+        return jnp.dot(packed, synthesis_ref[...], preferred_element_type=jnp.float32)
 
     def block(rank, size):
         return pl.ds(pl.multiple_of(rank * size, size), size)
@@ -405,7 +437,7 @@
     order = sorted(range(1, groups), key=lambda step: -min(step, groups - step))
     tile = 8
 
-    def back_group(b, group, grad_ref, fresh):
+    def back_group(b, group, grad_ref, fresh, last):
         here = slice(b * chans, (b + 1) * chans)
         for k in range(kept_here):
             values = grad_ref[k]
@@ -425,11 +457,18 @@
                     for i, factor in enumerate(factors):
                         term = w * factor
                         sums[c][i] = term if sums[c][i] is None else sums[c][i] + term
-            into = pl.ds(pl.multiple_of(first, tile), tile)
-            for i, acc_ref in ((0, accp_ref), (1, accq_ref)):
-                rows = [jnp.sum(sums[c][i], axis=0, keepdims=True) for c in range(tile)]
-                total = jnp.concatenate(rows, axis=0)
-                acc_ref[b, k, into, :] = total if fresh else acc_ref[b, k, into, :] + total
+            for i in range(2):
+                for c in range(tile):
+                    if not fresh:
+                        sums[c][i] = sums[c][i] + acc_ref[b, at, i, c]
+                    if not last:
+                        acc_ref[b, at, i, c] = sums[c][i]
+            if last:
+                p, q = (row_sums([pair[i] for pair in sums]) for i in range(2))
+                into = pl.ds(pl.multiple_of(first, tile), tile)
+                few_ref[6, b, k, into, :] = jnp.where(
+                    even_lanes(p), p + next_lane(p), prev_lane(q) - q
+                )
 
     def flow(b):
         for copy in load_field[b * rows_here:(b + 1) * rows_here]:
@@ -438,6 +477,8 @@
         if b == 0:
             pl.semaphore_wait(barrier, ranks - 1 + groups - 1)
         spread(0, b)
+        if b == samples - 1:
+            fill_synthesis()
         yield
         transform(0, b, fwd_ref, scale_fwd)
         yield
@@ -490,61 +531,88 @@
             copy.start()
             copies.append(copy)
         at_end.extend(copy.wait_send for copy in copies)
-        back_group(b, mine, own, True)
-        yield
-        for step in sorted(order, key=lambda step: min(step, groups - step)):
+        back_group(b, mine, own, True, groups == 1)
+        yield
+        near = sorted(order, key=lambda step: min(step, groups - step))
+        for step in near:
             copies[order.index(step)].wait_recv()
             source = lax.rem(mine + groups - step, groups)
-            back_group(b, source, gall_ref.at[b, source], False)
-        for k in range(kept_here):
-            p, q = accp_ref[b, k], accq_ref[b, k]
-            few_ref[6, b, k] = jnp.where(even_lanes(p), p + next_lane(p), prev_lane(q) - q)
+            back_group(b, source, gall_ref.at[b, source], False, step == near[-1])
         spread(6, b)
         yield
         transform(6, b, inv_ref, scale_fwd)
         yield
         few = collected(7, b)
         gfield_ref[b] = synth_cols(few[...]).reshape(rows_here, chans, width)
+
+    flows = [flow(b) for b in range(samples)]
+    stages = 11
+    lag = [[0, 1, 2], [3, 4], [5], [6], [7], [8, 9], [10]]
+    follow = [[0, 1, 2], [3], [4], [5], [6, 7], [8], [9, 10]]
+    assert sum(map(len, lag)) == sum(map(len, follow)) == stages
+    turns = [0, 1, 0, 1, 0, 1]
+    for ahead, behind in zip(lag[1:], follow[1:]):
+        turns += [0] * len(ahead) + [1] * len(behind)
+    for turn in turns:
+        for one in flows[:1] if turn == 0 else flows[1:]:
+            next(one, None)
+    for act in at_end:
+        act()
+
+
+def output_kernel(
+    same_ref, cross_ref, grads_ref, gswap_ref, rows_hbm, gfield_hbm, gweight_hbm,
+    gweight_ref, field_sem, weight_sem,
+):
+    samples, rows_here, chans = rows_hbm.shape[:3]
+    groups, kept_here = grads_ref.shape[:2]
+    tile, together, count = 8, 2, 8
+    copies = []
+    for b in range(samples):
         for h in range(rows_here):
             copy = pltpu.make_async_copy(
-                gfield_ref.at[b, h], gfield_hbm.at[b, :, h, :], field_sem.at[0, b, h]
+                rows_hbm.at[b, h], gfield_hbm.at[b, :, h, :], field_sem.at[b, h]
             )
             copy.start()
-            at_end.append(copy.wait)
-
-    flows = [flow(b) for b in range(samples)]
-    while flows:
-        for one in list(flows):
-            if next(one, flows) is flows:
-                flows.remove(one)
-    for act in at_end:
-        act()
-
-
-def weight_kernel(chans, samples, same_ref, cross_ref, grads_ref, gswap_ref, out_ref):
-    tile, together = 8, 2
-    count = out_ref.shape[1]
-    first = pl.program_id(1) * count
-
-    for c in range(0, count, together):
-        same, cross = [
-            [
-                [ref[0, pl.ds(b * chans + first + c + i, 1), :] for b in range(samples)]
-                for i in range(together)
+            copies.append(copy)
+
+    def weight_copy(at):
+        k, first = at // (chans // count), at % (chans // count) * count
+        here = pl.ds(first, count)
+        return pltpu.make_async_copy(
+            gweight_ref.at[k, here], gweight_hbm.at[k, here], weight_sem.at[at]
+        )
+
+    @pl.loop(0, kept_here * (chans // count))
+    def _(at):
+        k, first = at // (chans // count), at % (chans // count) * count
+        for c in range(0, count, together):
+            same, cross = [
+                [
+                    [ref[k, pl.ds(b * chans + first + c + i, 1), :] for b in range(samples)]
+                    for i in range(together)
+                ]
+                for ref in (same_ref, cross_ref)
             ]
-            for ref in (same_ref, cross_ref)
-        ]
-        for group in range(grads_ref.shape[0]):
-            for o in range(0, chans, tile):
-                rows = [slice(b * chans + o, b * chans + o + tile) for b in range(samples)]
-                plain = [grads_ref[group, 0, row, :] for row in rows]
-                turned = [gswap_ref[group, 0, row, :] for row in rows]
-                at = group * chans + o
-                for i in range(together):
-                    total = plain[0] * same[i][0] + turned[0] * cross[i][0]
-                    for b in range(1, samples):
-                        total = total + plain[b] * same[i][b] + turned[b] * cross[i][b]
-                    out_ref[0, c + i, at:at + tile, :] = total
+            for group in range(groups):
+                for o in range(0, chans, tile):
+                    rows = [slice(b * chans + o, b * chans + o + tile) for b in range(samples)]
+                    plain = [grads_ref[group, k, row, :] for row in rows]
+                    turned = [gswap_ref[group, k, row, :] for row in rows]
+                    out = group * chans + o
+                    for i in range(together):
+                        total = plain[0] * same[i][0] + turned[0] * cross[i][0]
+                        for b in range(1, samples):
+                            total = total + plain[b] * same[i][b] + turned[b] * cross[i][b]
+                        gweight_ref[k, first + c + i, out:out + tile, :] = total
+        weight_copy(at).start()
+
+    @pl.loop(0, kept_here * (chans // count))
+    def _(at):
+        weight_copy(at).wait()
+
+    for copy in copies:
+        copy.wait()
 
 
 def kernel_fits(ranks, groups, field, weight, mode_rows, bias):
@@ -569,32 +637,31 @@
     f32, bf16, i32 = jnp.float32, jnp.bfloat16, jnp.int32
     sizes = (samples, chans, rows_here, width, kept, ranks, groups, lanes)
     vmem = pl.BlockSpec(memory_space=pltpu.VMEM)
-    hbm = pl.BlockSpec(memory_space=pl.ANY)
+    hbm = pl.BlockSpec(memory_space=pltpu.HBM)
     modes = (kept_here, pairs, lanes)
     slab = (kept_here, chans, lanes)
     by_row = (samples, rows_here, chans, width)
     dma = pltpu.SemaphoreType.DMA
-    gfield, same, cross, grads, gswap = pl.pallas_call(
+    rows, same, cross, grads, gswap = pl.pallas_call(
         functools.partial(layer_kernel, sizes),
         out_shape=(
-            jax.ShapeDtypeStruct(field.shape, f32),
+            jax.ShapeDtypeStruct(by_row, f32),
             jax.ShapeDtypeStruct(modes, f32),
             jax.ShapeDtypeStruct(modes, f32),
             jax.ShapeDtypeStruct((groups,) + modes, f32),
             jax.ShapeDtypeStruct((groups,) + modes, f32),
         ),
         in_specs=[hbm] * 6,
-        out_specs=(hbm,) + (vmem,) * 4,
+        out_specs=(vmem,) * 5,
         scratch_shapes=[
             pltpu.VMEM(weight.shape, f32),
-            pltpu.VMEM(by_row, f32),
             pltpu.VMEM(by_row, f32),
             pltpu.VMEM(by_row, f32),
             pltpu.VMEM((1, bias.shape[0]), f32),
             pltpu.VMEM((1, lanes // 2), i32),
             pltpu.VMEM((1, kept), i32),
-            pltpu.VMEM((width, lanes), bf16),
-            pltpu.VMEM((width, lanes), bf16),
+            pltpu.VMEM((width, 2 * lanes), bf16),
+            pltpu.VMEM((3 * lanes, width), bf16),
             pltpu.VMEM((kept, 6 * grid_rows), bf16),
             pltpu.VMEM((grid_rows, 6 * kept), bf16),
             pltpu.VMEM((6 * kept, own_chans * lanes), bf16),
@@ -603,8 +670,7 @@
             pltpu.VMEM((samples, groups - 1) + slab, f32),
             pltpu.VMEM((samples, groups - 1) + slab, f32),
             pltpu.VMEM((samples, groups) + slab, f32),
-            pltpu.VMEM((samples,) + slab, f32),
-            pltpu.VMEM((samples,) + slab, f32),
+            pltpu.VMEM((samples, kept_here * chans // 8, 2, 8, 8, lanes), f32),
             dma((4,)),
             dma((2, samples, rows_here)),
             dma((8, ranks)),
@@ -621,17 +687,20 @@
         mode_cols.reshape(1, lanes // 2),
         mode_rows.reshape(1, kept),
     )
-    count = 8
-    one = pl.BlockSpec((1, pairs, lanes), lambda k, c: (k, 0, 0))
-    every = pl.BlockSpec((groups, 1, pairs, lanes), lambda k, c: (0, k, 0, 0))
-    gweight = pl.pallas_call(
-        functools.partial(weight_kernel, chans, samples),
-        out_shape=jax.ShapeDtypeStruct(weight.shape, f32),
-        grid=(kept_here, chans // count),
-        in_specs=[one, one, every, every],
-        out_specs=pl.BlockSpec((1, count) + weight.shape[2:], lambda k, c: (k, c, 0, 0)),
+    gfield, gweight = pl.pallas_call(
+        output_kernel,
+        out_shape=(
+            jax.ShapeDtypeStruct(field.shape, f32), jax.ShapeDtypeStruct(weight.shape, f32),
+        ),
+        in_specs=[vmem] * 4 + [pl.BlockSpec(memory_space=pl.ANY)],
+        out_specs=(hbm, hbm),
+        scratch_shapes=[
+            pltpu.VMEM(weight.shape, f32),
+            dma((samples, rows_here)),
+            dma((kept_here * chans // 8,)),
+        ],
         compiler_params=pltpu.CompilerParams(vmem_limit_bytes=32 * 1024 * 1024),
-    )(same, cross, grads, gswap)
+    )(same, cross, grads, gswap, rows)
     return gfield, gweight
 
 

time: 72.9 us -> 73.4 us (level)
  Pallas kernels: 68.6 us -> 69.4 us
    pallas_call x1, Pallas kernels: 61 us -> 65.6 us  [kernel_body(): pl.pallas_call(functools.partial(layer_kernel, sizes), out_shape=(jax.Sha...]
    pallas_call x1, Pallas kernels: 7.66 us -> 3.81 us  [kernel_body(): pl.pallas_call(output_kernel, out_shape=(jax.ShapeDtypeStruct(field.shape...]
    unnamed x9 -> x8, local copies, waits for them, and re-layouts: 2.93 us -> 3.18 us
where the time goes in v1:
time: 73.4 us; the launch traced here: 73.3 us
  Pallas kernels  69.4 us (95%)
  local copies, waits for them, and re-layouts  3.18 us (4%)
    pallas_call x1, Pallas kernels, kernel_body(): pl.pallas_call(functools.partial(layer_kernel, sizes), out_shape=(jax.Sha...  65.6 us
    pallas_call x1, Pallas kernels, kernel_body(): pl.pallas_call(output_kernel, out_shape=(jax.ShapeDtypeStruct(field.shape...  3.81 us
    unnamed x8, local copies, waits for them, and re-layouts  3.18 us

profile of v1, /device:TPU:17, one launch (start us, length us, event | category | flops | bytes accessed | tf_op | source)
XLA Modules:
  0.0 73.3 jit_solution(12908829137123760298)
XLA Ops:
  0.6 0.0 copy-start.1
  0.6 0.6 copy-done.1
  1.3 0.0 copy-start.2
  1.3 0.7 copy-done.2
  1.9 0.0 copy-start.3
  1.9 0.7 copy-done.3
  2.6 65.6 %shard_map.77 = (f32[2,4,32,1024]{3,2,1,0:T(8,128)}, f32[4,64,128]{2,1,0:T(8,128)S(1)}, f32[4,64,128]{2,1,0:T(8,128)S(1)}, f32[4,4,64,128]{3,2,1,0:T(8,128)S(1)}, f32[4,4,64,128]{3,2,1,0:T(8,128)S(1)}) custom-call(f32[2,32,4,1024]{3,2,1,0:T(4,128)} %field_hbm.1, f32[2,32,4,1024]{3,2,1,0:T(4,128)} %cot_hbm.1, f32[4,32,128,128]{3,2,1,0:T(8,128)} %weight_hbm.1, ...), custom_call_target="tpu_custom_call" | custom-call | tf_op jit(solution)/shard_map/pallas_call | solution.py:645
  68.2 0.0 copy-start
  68.2 1.2 %copy-done = f32[2,4,32,1024]{3,2,1,0:T(8,128)S(1)} copy-done((f32[2,4,32,1024]{3,2,1,0:T(8,128)S(1)}, f32[2,4,32,1024]{3,2,1,0:T(8,128)}, u32[]{:S(2)}) %copy-start) | copy-done | bytes 1048600
  69.4 3.8 %shard_map.78 = (f32[2,32,4,1024]{3,2,1,0:T(4,128)}, f32[4,32,128,128]{3,2,1,0:T(8,128)}) custom-call(f32[4,64,128]{2,1,0:T(8,128)S(1)} %get-tuple-element.7.same_ref, f32[4,64,128]{2,1,0:T(8,128)S(1)} %get-tuple-element.8.cross_ref, f32[4,4,64,128]{3,2,1,0:T(8,128)S(1)} %get-tuple-element.9.grads_ref, f32[4,4,64,128]{3,2,1,0:T(8,128)S(1)} %get-tuple-element.10.gswap_ref, ...), custom_call_target="tpu_custom_call" | custom-call | tf_op jit(solution)/shard_map/pallas_call | solution.py:690
Async XLA Ops:
  0.6 0.7 copy-start.1
  1.3 0.7 copy-start.2
  1.9 0.7 copy-start.3
  68.2 1.2 %copy-start = (f32[2,4,32,1024]{3,2,1,0:T(8,128)S(1)}, f32[2,4,32,1024]{3,2,1,0:T(8,128)}, u32[]{:S(2)}) copy-start(f32[2,4,32,1024]{3,2,1,0:T(8,128)} %get-tuple-element.11.rows_hbm) | copy-start | bytes 3145732

commit v2 on v1

--- a/solution.py
+++ b/solution.py
@@ -183,9 +183,9 @@
 
 
 def layer_kernel(
-    sizes, field_hbm, cot_hbm, weight_hbm, bias_hbm, colmode_hbm, rowmode_hbm,
-    gfield_ref, same_ref, cross_ref, grads_ref, gswap_ref,
-    weight_ref, field_ref, cot_ref, bias_ref, colmode_ref, rowmode_ref,
+    sizes, field_hbm, cot_hbm, weight_hbm, small_hbm,
+    gfield_ref, same_ref, cross_ref, grads_ref,
+    gswap_ref, weight_ref, field_ref, cot_ref, small_ref,
     analysis_ref, synthesis_ref, fwd_ref, inv_ref, stack_ref,
     few_ref, many_ref, part_ref, arrive_ref, gall_ref, acc_ref,
     local_sem, field_sem, send_sem, recv_sem, ch_send, ch_recv,
@@ -214,13 +214,8 @@
     for step in range(1, groups):
         pl.semaphore_signal(barrier, inc=1, device_id=(me, group_at(step)), device_id_type=mesh_ids)
 
-    loads = []
-    for at, (source, target) in enumerate((
-        (colmode_hbm, colmode_ref), (rowmode_hbm, rowmode_ref), (bias_hbm, bias_ref),
-    )):
-        load = pltpu.make_async_copy(source, target, local_sem.at[at])
-        load.start()
-        loads.append(load)
+    load_small = pltpu.make_async_copy(small_hbm, small_ref, local_sem.at[0])
+    load_small.start()
 
     def row_copies(source, target, kind):
         found = []
@@ -234,11 +229,10 @@
         return found
 
     load_field = row_copies(field_hbm, field_ref, 0)
-    load_weight = pltpu.make_async_copy(weight_hbm, weight_ref, local_sem.at[3])
+    load_weight = pltpu.make_async_copy(weight_hbm, weight_ref, local_sem.at[1])
     load_weight.start()
     load_cot = row_copies(cot_hbm, cot_ref, 1)
-    for load in loads:
-        load.wait()
+    load_small.wait()
 
     def as_column(values):
         count = values.shape[1]
@@ -251,9 +245,9 @@
         row = lax.broadcasted_iota(jnp.int32, (column.shape[0], index.shape[1]), 0)
         return jnp.sum(jnp.where(row == index, column, 0.0), axis=0, keepdims=True).astype(jnp.int32)
 
-    col_column = as_column(colmode_ref[...])
+    col_column = as_column(small_ref[1:2, :lanes // 2])
     col_lanes = pick(col_column, lax.broadcasted_iota(jnp.int32, (1, lanes), 1) // 2)
-    row_column = as_column(rowmode_ref[...])
+    row_column = as_column(small_ref[2:3, :kept])
     row_lanes = pick(row_column, lax.broadcasted_iota(jnp.int32, (1, 6 * kept), 1) % kept)
     row_column = row_column.astype(jnp.int32)
     chunk = 128
@@ -297,10 +291,10 @@
     turn = spot // kept % 2 * (grid_rows // 4)
     row = lax.broadcasted_iota(jnp.int32, (grid_rows, 6 * kept), 0)
     inv_ref[...] = packed_table(row_lanes * row + turn, grid_rows)
-    whole = bias_ref.shape[1]
+    whole = small_ref.shape[1]
     out_chan = mine * chans + lax.broadcasted_iota(jnp.int32, (flat_rows, whole), 0) % chans
     picked = lax.broadcasted_iota(jnp.int32, (flat_rows, whole), 1) == out_chan
-    bias_rows = jnp.sum(jnp.where(picked, bias_ref[...], 0.0), axis=1, keepdims=True)
+    bias_rows = jnp.sum(jnp.where(picked, small_ref[0:1, :], 0.0), axis=1, keepdims=True)
 
     def analyze_cols(values):
         high, low = split_bf16(values.reshape(flat_rows, width))
@@ -546,23 +540,16 @@
         gfield_ref[b] = synth_cols(few[...]).reshape(rows_here, chans, width)
 
     flows = [flow(b) for b in range(samples)]
-    stages = 11
-    lag = [[0, 1, 2], [3, 4], [5], [6], [7], [8, 9], [10]]
-    follow = [[0, 1, 2], [3], [4], [5], [6, 7], [8], [9, 10]]
-    assert sum(map(len, lag)) == sum(map(len, follow)) == stages
-    turns = [0, 1, 0, 1, 0, 1]
-    for ahead, behind in zip(lag[1:], follow[1:]):
-        turns += [0] * len(ahead) + [1] * len(behind)
-    for turn in turns:
-        for one in flows[:1] if turn == 0 else flows[1:]:
+    for _ in range(11):
+        for one in flows:
             next(one, None)
     for act in at_end:
         act()
 
 
 def output_kernel(
-    same_ref, cross_ref, grads_ref, gswap_ref, rows_hbm, gfield_hbm, gweight_hbm,
-    gweight_ref, field_sem, weight_sem,
+    same_ref, cross_ref, grads_ref, rows_hbm, gfield_hbm, gweight_hbm,
+    gweight_ref, gswap_ref, field_sem, weight_sem,
 ):
     samples, rows_here, chans = rows_hbm.shape[:3]
     groups, kept_here = grads_ref.shape[:2]
@@ -575,6 +562,11 @@
             )
             copy.start()
             copies.append(copy)
+
+    @pl.loop(0, kept_here)
+    def _(k):
+        for group in range(groups):
+            gswap_ref[group, k] = swap_pairs(grads_ref[group, k])
 
     def weight_copy(at):
         k, first = at // (chans // count), at % (chans // count) * count
@@ -634,7 +626,11 @@
     kept_here = kept // ranks
     pairs = samples * chans
     own_chans = pairs // ranks
-    f32, bf16, i32 = jnp.float32, jnp.bfloat16, jnp.int32
+    f32, bf16 = jnp.float32, jnp.bfloat16
+    small = jnp.stack([
+        jnp.pad(values.astype(f32), (0, bias.shape[0] - values.shape[0]))
+        for values in (bias, mode_cols, mode_rows)
+    ])
     sizes = (samples, chans, rows_here, width, kept, ranks, groups, lanes)
     vmem = pl.BlockSpec(memory_space=pltpu.VMEM)
     hbm = pl.BlockSpec(memory_space=pltpu.HBM)
@@ -642,24 +638,22 @@
     slab = (kept_here, chans, lanes)
     by_row = (samples, rows_here, chans, width)
     dma = pltpu.SemaphoreType.DMA
-    rows, same, cross, grads, gswap = pl.pallas_call(
+    rows, same, cross, grads = pl.pallas_call(
         functools.partial(layer_kernel, sizes),
         out_shape=(
             jax.ShapeDtypeStruct(by_row, f32),
             jax.ShapeDtypeStruct(modes, f32),
             jax.ShapeDtypeStruct(modes, f32),
             jax.ShapeDtypeStruct((groups,) + modes, f32),
-            jax.ShapeDtypeStruct((groups,) + modes, f32),
         ),
-        in_specs=[hbm] * 6,
-        out_specs=(vmem,) * 5,
+        in_specs=[hbm] * 4,
+        out_specs=(vmem,) * 4,
         scratch_shapes=[
+            pltpu.VMEM((groups,) + modes, f32),
             pltpu.VMEM(weight.shape, f32),
             pltpu.VMEM(by_row, f32),
             pltpu.VMEM(by_row, f32),
-            pltpu.VMEM((1, bias.shape[0]), f32),
-            pltpu.VMEM((1, lanes // 2), i32),
-            pltpu.VMEM((1, kept), i32),
+            pltpu.VMEM(small.shape, f32),
             pltpu.VMEM((width, 2 * lanes), bf16),
             pltpu.VMEM((3 * lanes, width), bf16),
             pltpu.VMEM((kept, 6 * grid_rows), bf16),
@@ -671,7 +665,7 @@
             pltpu.VMEM((samples, groups - 1) + slab, f32),
             pltpu.VMEM((samples, groups) + slab, f32),
             pltpu.VMEM((samples, kept_here * chans // 8, 2, 8, 8, lanes), f32),
-            dma((4,)),
+            dma((2,)),
             dma((2, samples, rows_here)),
             dma((8, ranks)),
             dma((8, ranks)),
@@ -682,25 +676,23 @@
             collective_id=0, has_side_effects=True, vmem_limit_bytes=52 * 1024 * 1024
         ),
     )(
-        field, cotangent, weight,
-        bias.reshape(1, bias.shape[0]),
-        mode_cols.reshape(1, lanes // 2),
-        mode_rows.reshape(1, kept),
+        field, cotangent, weight, small,
     )
     gfield, gweight = pl.pallas_call(
         output_kernel,
         out_shape=(
             jax.ShapeDtypeStruct(field.shape, f32), jax.ShapeDtypeStruct(weight.shape, f32),
         ),
-        in_specs=[vmem] * 4 + [pl.BlockSpec(memory_space=pl.ANY)],
+        in_specs=[vmem] * 3 + [pl.BlockSpec(memory_space=pl.ANY)],
         out_specs=(hbm, hbm),
         scratch_shapes=[
             pltpu.VMEM(weight.shape, f32),
+            pltpu.VMEM(grads.shape, f32),
             dma((samples, rows_here)),
             dma((kept_here * chans // 8,)),
         ],
         compiler_params=pltpu.CompilerParams(vmem_limit_bytes=32 * 1024 * 1024),
-    )(same, cross, grads, gswap, rows)
+    )(same, cross, grads, rows)
     return gfield, gweight
 
 

time: 73.4 us -> 68.5 us (0.933)
  Pallas kernels: 69.4 us -> 65.2 us
  local copies, waits for them, and re-layouts: 3.18 us -> 0.01 us
  other arithmetic: 0 us -> 1.98 us
    pallas_call x1, Pallas kernels: 65.6 us -> 61.1 us  [kernel_body(): pl.pallas_call(functools.partial(layer_kernel, sizes), out_shape=(jax.Sha...]
    unnamed x8 -> x0, local copies, waits for them, and re-layouts: 3.18 us -> none
    convert_element_type x0 -> x2, other arithmetic: none -> 1.32 us  [kernel_body(): values.astype(f32)]
where the time goes in v2:
time: 68.5 us; the launch traced here: 67.9 us
  Pallas kernels  65.2 us (95%)
  other arithmetic  1.98 us (3%)
    pallas_call x1, Pallas kernels, kernel_body(): pl.pallas_call(functools.partial(layer_kernel, sizes), out_shape=(jax.Sha...  61.1 us
    pallas_call x1, Pallas kernels, kernel_body(): pl.pallas_call(output_kernel, out_shape=(jax.ShapeDtypeStruct(field.shape...  4.19 us

profile of v2, /device:TPU:17, one launch (start us, length us, event | category | flops | bytes accessed | tf_op | source)
XLA Modules:
  0.0 67.9 jit_solution(16337390053862951279)
XLA Ops:
  0.6 0.7 convert_element_type.11
  1.3 0.7 convert_element_type.10
  2.0 0.7 pad_maximum_fusion.small_hbm
  2.6 61.1 %shard_map.77 = (f32[2,4,32,1024]{3,2,1,0:T(8,128)S(1)}, f32[4,64,128]{2,1,0:T(8,128)S(1)}, f32[4,64,128]{2,1,0:T(8,128)S(1)}, f32[4,4,64,128]{3,2,1,0:T(8,128)S(1)}) custom-call(f32[2,32,4,1024]{3,2,1,0:T(4,128)} %field_hbm.1, f32[2,32,4,1024]{3,2,1,0:T(4,128)} %cot_hbm.1, f32[4,32,128,128]{3,2,1,0:T(8,128)} %weight_hbm.1, ...), custom_call_target="tpu_custom_call" | custom-call | tf_op jit(solution)/shard_map/pallas_call | solution.py:641
  63.7 4.2 %shard_map.78 = (f32[2,32,4,1024]{3,2,1,0:T(4,128)}, f32[4,32,128,128]{3,2,1,0:T(8,128)}) custom-call(f32[4,64,128]{2,1,0:T(8,128)S(1)} %get-tuple-element.6.same_ref, f32[4,64,128]{2,1,0:T(8,128)S(1)} %get-tuple-element.7.cross_ref, f32[4,4,64,128]{3,2,1,0:T(8,128)S(1)} %get-tuple-element.8.grads_ref, f32[2,4,32,1024]{3,2,1,0:T(8,128)S(1)} %get-tuple-element.9.rows_hbm), custom_call_target="tpu_custom_call" | custom-call | tf_op jit(solution)/shard_map/pallas_call | solution.py:681
  (1 shorter events, 0.0 us)
